TPU v7x, 256 devices: a whole 4x4x8 slice. The times are simulated.
256 devices in a mesh: prow: 16 (over z, core), pcol: 16 (over y, x).
Axes of the slice: x: 4, y: 4, z: 8, core: 2. Of those that a mesh axis runs over, the one named last changes fastest.
Arguments:
- panel_pre: bfloat16 [31, 16, 256, 1, 16, 256], P(None, 'prow', None, None, 'pcol'), may hold values from -0.015625 to 0.015625
- tail_panel: bfloat16 [1, 16, 256, 1, 16, 256], P(None, 'prow', None, None, 'pcol'), may hold values from -0.09375 to 0.09375
- earlier: bfloat16 [32, 31, 16, 256], P('pcol', None, 'prow'), may hold values from -6 to 6
- right_side: float32 [32, 1, 16, 256], P(None, None, 'pcol'), may hold values from -6 to 6
- inverses: float32 [1, 16, 256, 1024], P(None, 'pcol'), may hold values from -0.08 to 1.08
Outputs:
- solution: float32 [32, 1, 16, 256], P(None, None, 'pcol')
All inputs are finite; a program needn't handle non-finite values.
Results may differ from a plain program's by a relative error of at most 0.0021.
Values may be sent and summed in bfloat16 or wider, within the bound.
A program may use at most 64 MiB of HBM per device.

v0:
```python
import jax
import jax.numpy as jnp
from jax import lax
from jax.sharding import PartitionSpec as P


def local(panel_pre, tail_panel, earlier, right_side, inverses):
    row_index = lax.axis_index("prow")
    col_index = lax.axis_index("pcol")
    col_count = lax.axis_size("pcol")
    count_rhs = right_side.shape[0]
    turns_cols = panel_pre.shape[3]
    tile_width = panel_pre.shape[5]
    turns_pre = panel_pre.shape[0]
    turns_tail = tail_panel.shape[0]
    block_width = inverses.shape[3]
    local_cols = turns_cols * tile_width
    total_cols = local_cols * col_count
    local_pre = panel_pre.reshape(turns_pre * tile_width, local_cols)
    known_rows = earlier.reshape(earlier.shape[0], turns_pre * tile_width)
    local_tail = tail_panel.reshape(turns_tail * tile_width, local_cols)
    local_inv = inverses.reshape(local_cols, block_width)
    base_rhs = right_side.reshape(count_rhs, local_cols)
    prior_part = jnp.dot(
        lax.all_gather(known_rows, "pcol", axis=0, tiled=True),
        local_pre,
        preferred_element_type=jnp.float32,
    )
    prior = lax.psum(prior_part, "prow")
    base = base_rhs - prior
    col_global = (
        (jnp.arange(turns_cols, dtype=jnp.int32)[:, None] * col_count + col_index) * tile_width
        + jnp.arange(tile_width, dtype=jnp.int32)[None, :]
    ).reshape(local_cols)
    col_block = col_global // block_width
    solved = jnp.zeros((count_rhs, total_cols), jnp.float32)
    for step in range(total_cols // block_width):
        rounded = solved.astype(jnp.bfloat16)
        row_groups = rounded.reshape(count_rhs, turns_tail, lax.axis_size("prow"), tile_width)
        mine = lax.dynamic_slice_in_dim(row_groups, row_index, 1, 2).reshape(
            count_rhs, turns_tail * tile_width
        )
        partial_update = jnp.dot(mine, local_tail, preferred_element_type=jnp.float32)
        update = lax.psum(partial_update, "prow")
        remain = base - update
        masked = jnp.where((col_block == step)[None, :], remain, jnp.zeros_like(remain))
        partial_x = jnp.dot(masked, local_inv, precision=lax.Precision.HIGHEST)
        block_x = lax.psum(partial_x, "pcol")
        solved = solved.at[:, step * block_width : (step + 1) * block_width].set(block_x)
    grouped = solved.reshape(count_rhs, turns_cols, col_count, tile_width)
    return lax.dynamic_slice_in_dim(grouped, col_index, 1, 2)


def solution(mesh):
    in_specs = (
        P(None, "prow", None, None, "pcol", None),
        P(None, "prow", None, None, "pcol", None),
        P("pcol", None, "prow", None),
        P(None, None, "pcol", None),
        P(None, "pcol", None, None),
    )
    out_specs = P(None, None, "pcol", None)
    return jax.shard_map(local, mesh=mesh, in_specs=in_specs, out_specs=out_specs, check_vma=False)
```

profile of v0, /device:TPU:25, one launch (start us, length us, event | category | flops | bytes accessed | tf_op | source)
XLA Modules:
  0.0 659.4 jit_solution(10268724816689693890)
XLA Ops:
  6.5 18.3 %all-gather = bf16[16,2,7936]{2,1,0:T(2,128)(2,1)S(1)} all-gather(bf16[1,2,7936]{2,1,0:T(2,128)(2,1)} %bitcast.60), channel_id=1, replica_groups=mesh['prow'=16,'pcol'=16] {'pcol'}, dimensions={0}, use_global_device_ids=true | all-gather | bytes 539648 | tf_op jit(solution)/shard_map/all_gather | solution.py:25
  25.1 1.7 fusion.15
  26.7 3.6 fusion.39
  30.4 106.2 %all-reduce.16.cloned.1.call-done = (f32[32,256]{1,0:T(8,128)}, f32[32,256]{1,0:T(8,128)}) async-done(((f32[32,256]{1,0:T(8,128)}, f32[32,256]{1,0:T(8,128)}), (f32[32,256]{1,0:T(8,128)}, f32[32,256]{1,0:T(8,128)})) %all-reduce.16.cloned.1.call-update) | async-done | bytes 65552 | tf_op jit(solution)/shard_map/psum | solution.py:29
  136.6 0.8 bitcast_subtract_fusion
  137.3 2.1 fusion.6
  139.5 0.6 compare_reduce_fusion.2
  140.2 88.2 %all-reduce.8.cloned.1.call-done = f32[32,1024]{1,0:T(8,128)} async-done(((f32[32,1024]{1,0:T(8,128)}), f32[32,1024]{1,0:T(8,128)}) %all-reduce.8.cloned.1.call-update) | async-done | bytes 131088 | tf_op jit(solution)/shard_map/psum | solution.py:48
  228.4 1.6 broadcast_select_fusion
  230.3 45.5 %psum.66 = f32[32,256]{1,0:T(8,128)S(1)} all-reduce(f32[32,256]{1,0:T(8,128)S(1)} %fusion.13), channel_id=1, replica_groups=mesh['prow'=16,'pcol'=16] {'prow'}, use_global_device_ids=true, to_apply=%region_5.6 | all-reduce | flops 8192 | bytes 65536 | tf_op jit(solution)/shard_map/psum | solution.py:44
  275.7 1.4 fusion.4
  277.1 0.6 compare_reduce_fusion.1
  277.8 91.5 %all-reduce.10.cloned.1.call-done = f32[32,1024]{1,0:T(8,128)} async-done(((f32[32,1024]{1,0:T(8,128)}), f32[32,1024]{1,0:T(8,128)}) %all-reduce.10.cloned.1.call-update) | async-done | bytes 131088 | tf_op jit(solution)/shard_map/psum | solution.py:48
  369.3 1.6 select_dynamic-update-slice_fusion
  371.2 45.5 %psum.68 = f32[32,256]{1,0:T(8,128)S(1)} all-reduce(f32[32,256]{1,0:T(8,128)S(1)} %fusion.11), channel_id=1, replica_groups=mesh['prow'=16,'pcol'=16] {'prow'}, use_global_device_ids=true, to_apply=%region_8.9 | all-reduce | flops 8192 | bytes 65536 | tf_op jit(solution)/shard_map/psum | solution.py:44
  416.6 1.4 fusion.2
  418.0 0.6 compare_reduce_fusion
  418.7 91.5 %all-reduce.12.cloned.1.call-done = f32[32,1024]{1,0:T(8,128)} async-done(((f32[32,1024]{1,0:T(8,128)}), f32[32,1024]{1,0:T(8,128)}) %all-reduce.12.cloned.1.call-update) | async-done | bytes 131088 | tf_op jit(solution)/shard_map/psum | solution.py:48
  510.2 1.6 fusion.8
  512.1 45.5 %psum.70 = f32[32,256]{1,0:T(8,128)S(1)} all-reduce(f32[32,256]{1,0:T(8,128)S(1)} %fusion.9), channel_id=1, replica_groups=mesh['prow'=16,'pcol'=16] {'prow'}, use_global_device_ids=true, to_apply=%region_10.11 | all-reduce | flops 8192 | bytes 65536 | tf_op jit(solution)/shard_map/psum | solution.py:44
  557.6 1.4 fusion
  558.9 92.2 %all-reduce.14.cloned.1.call-done = f32[32,1024]{1,0:T(8,128)} async-done(((f32[32,1024]{1,0:T(8,128)}), f32[32,1024]{1,0:T(8,128)}) %all-reduce.14.cloned.1.call-update) | async-done | bytes 131088 | tf_op jit(solution)/shard_map/psum | solution.py:48
  651.2 0.9 constant_dynamic-update-slice_fusion
  652.3 0.7 constant_dynamic-slice_fusion
  (35 shorter events, 1.5 us)
Async XLA Ops:
  6.5 130.8 %copy-start = (f32[1,1,256,1024]{3,2,1,0:T(8,128)S(1)}, f32[1,1,256,1024]{3,2,1,0:T(8,128)}, u32[]{:S(2)}) copy-start(f32[1,1,256,1024]{3,2,1,0:T(8,128)} %param.17) | copy-start | bytes 3145732
  6.5 130.0 %copy-start.2 = (f32[32,1,1,256]{3,2,1,0:T(1,128)S(1)}, f32[32,1,1,256]{3,2,1,0:T(1,128)}, u32[]{:S(2)}) copy-start(f32[32,1,1,256]{3,2,1,0:T(1,128)} %param.16) | copy-start | bytes 98308
  6.5 130.0 %all-reduce.16.cloned.1.call-start = ((), (), s32[]{:S(2)}) async-start(), calls=%async_computation.4 | async-start | bytes 131072 | tf_op jit(solution)/shard_map/psum | solution.py:29
  24.9 205.2 %copy-start.1 = (bf16[1,1,256,1,1,256]{5,2,4,3,1,0:T(8,128)(2,1)S(1)}, bf16[1,1,256,1,1,256]{5,2,4,3,1,0:T(8,128)(2,1)}, u32[]{:S(2)}) copy-start(bf16[1,1,256,1,1,256]{5,2,4,3,1,0:T(8,128)(2,1)} %param.14) | copy-start | bytes 393220
  30.3 198.1 %all-reduce.8.cloned.1.call-start = ((), (), s32[]{:S(2)}) async-start(), calls=%async_computation | async-start | bytes 262144 | tf_op jit(solution)/shard_map/psum | solution.py:48
  139.4 229.9 %all-reduce.10.cloned.1.call-start = ((), (), s32[]{:S(2)}) async-start(), calls=%async_computation.1 | async-start | bytes 262144 | tf_op jit(solution)/shard_map/psum | solution.py:48
  277.1 233.1 %all-reduce.12.cloned.1.call-start = ((), (), s32[]{:S(2)}) async-start(), calls=%async_computation.2 | async-start | bytes 262144 | tf_op jit(solution)/shard_map/psum | solution.py:48
  418.0 233.2 %all-reduce.14.cloned.1.call-start = ((), (), s32[]{:S(2)}) async-start(), calls=%async_computation.3 | async-start | bytes 262144 | tf_op jit(solution)/shard_map/psum | solution.py:48
Sparse Core Ops, SparseCore 0:
  30.4 106.0 all-reduce.15
  140.1 88.2 all-reduce.7
  277.2 92.0 all-reduce.9
  418.1 92.0 all-reduce.11
  559.1 92.0 all-reduce.13
where the time goes:
time: 662 us; the launch traced here: 659 us
  waiting for transfers between devices  470 us (71%)
  blocking collectives  155 us (23%)
  between operations  13.3 us (2%)
  matrix products  11.8 us (2%)
  other arithmetic  7.51 us (1%)
    psum x4, waiting for transfers between devices, local(): block_x = lax.psum(partial_x, 'pcol')  363 us
    psum x3, blocking collectives, local(): update = lax.psum(partial_update, 'prow')  136 us
    psum x1, waiting for transfers between devices, local(): prior = lax.psum(prior_part, 'prow')  106 us
    all_gather x1, blocking collectives, local(): lax.all_gather(known_rows, 'pcol', axis=0, tiled=True)  18.3 us
  transfers between devices with their start and end apart: 5, of which 5 were waited for; matrix products, arithmetic and copies ran while one was open for 0% of the time, Pallas kernels for 0%

commit v1 on v0

v1 whole, which is shorter than its diff:
```python
import functools

import jax
import jax.numpy as jnp
from jax import lax
from jax.experimental import pallas as pl
from jax.experimental.pallas import tpu as pltpu
from jax.sharding import PartitionSpec as P

MESH = pl.DeviceIdType.MESH
F32 = jnp.float32
BF16 = jnp.bfloat16
CHUNKS = 4


def kernel(a_hbm, b_hbm, e_hbm, r_hbm, g_hbm, o_ref, e_ref, r_ref, abuf, ball, gbuf, h, part, pin, cxs, cxd, gp, xin, oin, ob, lsem, ysem, bsend, brecv, psem, csem, xsend, xrecv, osem, fsem):
    p = lax.axis_index("prow")
    col = lax.axis_index("pcol")
    z, core = p // 2, p % 2
    y, x = col // 4, col % 4
    turns = abuf.shape[0]

    def both(ref, sem):
        return pltpu.make_async_copy(ref, ref, sem)

    step = -(-turns // CHUNKS)
    loads = []
    for i in range(CHUNKS):
        size = min(step, turns - i * step)
        loads.append(pltpu.make_async_copy(a_hbm.at[pl.ds(i * step, size)], abuf.at[pl.ds(i * step, size)], lsem.at[i]))
    gload = [
        pltpu.make_async_copy(g_hbm.at[:, pl.ds(pl.multiple_of((core + 2 * i) * 256, 256), 256)], gbuf.at[i], lsem.at[CHUNKS + i])
        for i in range(2)
    ]
    load_y = pltpu.make_async_copy(e_hbm, e_ref, lsem.at[CHUNKS + 4])
    load_r = pltpu.make_async_copy(r_hbm.at[z], r_ref, lsem.at[CHUNKS + 5])
    own_y = pltpu.make_async_copy(e_hbm, h.at[:, col], lsem.at[CHUNKS + 2])
    own_b = pltpu.make_async_copy(b_hbm, ball.at[z], lsem.at[CHUNKS + 3])
    load_y.start()
    own_y.start()
    for c in loads:
        c.start()
    for c in gload:
        c.start()

    @pl.when(z < 2 * y)
    def _():
        own_b.start()

    load_r.start()

    cxs[...] = jnp.zeros_like(cxs)
    cxd[...] = jnp.zeros_like(cxd)

    barrier = pltpu.get_barrier_semaphore()
    for d in range(1, 16):
        pl.semaphore_signal(barrier, inc=1, device_id=(p, (col + d) % 16), device_id_type=MESH)
        pl.semaphore_signal(barrier, inc=1, device_id=((p + d) % 16, col), device_id_type=MESH)
    pl.semaphore_wait(barrier, 30)
    load_y.wait()

    for d in range(1, 16):
        pltpu.make_async_remote_copy(
            e_ref, h.at[:, col], ysem.at[0], ysem.at[1], device_id=(p, (col + d) % 16), device_id_type=MESH
        ).start()

    @pl.when(z < 2 * y)
    def _():
        for d in range(1, 8):
            pltpu.make_async_remote_copy(
                b_hbm, ball.at[z], bsend.at[0], brecv.at[z], device_id=((p + 2 * d) % 16, col), device_id_type=MESH
            ).start()

    own_y.wait()
    both(h.at[:, pl.ds(0, 15)], ysem.at[1]).wait()
    acc = jnp.zeros((32, 256), F32)
    for i in range(CHUNKS):
        loads[i].wait()
        for t in range(i * step, min((i + 1) * step, turns)):
            lhs = jnp.concatenate([h[2 * t].reshape(32, 128), h[2 * t + 1].reshape(32, 128)], axis=1)
            acc += jnp.dot(lhs, abuf[t], preferred_element_type=F32)
    part[...] = acc.reshape(8, 4, 256)

    for d in range(1, 16):
        to = (p + d) % 16
        pltpu.make_async_remote_copy(
            part.at[to // 2], pin.at[p], psem.at[0], psem.at[1], device_id=(to, col), device_id_type=MESH
        ).start()
    pin[p] = part[z]
    load_r.wait()
    rhs = r_ref[...].reshape(4, 256)
    both(pin.at[pl.ds(0, 15)], psem.at[1]).wait()
    base = rhs - jnp.sum(pin[...], axis=0)


    for i in range(3):

        @pl.when(y > i)
        def _():
            for k in range(2):

                @pl.when(z == 2 * i + k)
                def _():
                    own_b.wait()

                @pl.when(z != 2 * i + k)
                def _():
                    both(ball.at[2 * i + k], brecv.at[2 * i + k]).wait()

            both(xin.at[i], xrecv.at[i]).wait()
            solved = jnp.sum(xin[i], axis=0).astype(BF16)
            upd = cxs[...]
            for k in range(2):
                upd += jnp.dot(solved[k], ball[2 * i + k], preferred_element_type=F32)
            cxs[...] = upd

    @pl.when(y > 0)
    def _():
        swap = pltpu.make_async_remote_copy(
            cxs, cxd, csem.at[0], csem.at[1], device_id=(p + 1 - 2 * core, col), device_id_type=MESH
        )
        swap.start()
        swap.wait()

    update = cxs[...] + cxd[...]
    remain = base - update
    for i in range(2):
        gload[i].wait()
        gp[i] = jnp.dot(remain, gbuf[i], precision=lax.Precision.HIGHEST)

    for j in range(1, 4):

        @pl.when(y < j)
        def _():
            for k in range(4):
                pltpu.make_async_remote_copy(
                    gp, xin.at[y, x], xsend.at[j], xrecv.at[y], device_id=(p, 4 * j + k), device_id_type=MESH
                ).start()

    for k in range(2):
        to = core + 2 * k

        @pl.when(to != x)
        def _():
            pltpu.make_async_remote_copy(
                gp.at[k], oin.at[x], osem.at[k], osem.at[2], device_id=(p, 4 * y + to), device_id_type=MESH
            ).start()

    mine = x % 2 == core

    @pl.when(mine)
    def _():
        oin[x] = gp[x // 2]
        both(oin.at[pl.ds(0, 3)], osem.at[2]).wait()
        total = jnp.sum(oin[...], axis=0).reshape(4, 1, 256)
        ob[...] = total
        for d in range(1, 16):
            pltpu.make_async_remote_copy(
                ob, o_ref.at[z], fsem.at[0], fsem.at[1], device_id=((p + d) % 16, col), device_id_type=MESH
            ).start()
        o_ref[z] = total
        both(o_ref.at[pl.ds(0, 7)], fsem.at[1]).wait()
        both(o_ref.at[pl.ds(0, 7)], fsem.at[0]).wait()
        both(o_ref.at[pl.ds(0, 8)], fsem.at[0]).wait()

    @pl.when(jnp.logical_not(mine))
    def _():
        both(o_ref, fsem.at[1]).wait()

    both(h.at[:, pl.ds(0, 15)], ysem.at[0]).wait()
    both(pin.at[pl.ds(0, 15)], psem.at[0]).wait()

    @pl.when(z < 2 * y)
    def _():
        both(ball.at[pl.ds(0, 6)], bsend.at[0]).wait()
        both(ball.at[0], bsend.at[0]).wait()

        @pl.when(z >= 6)
        def _():
            own_b.wait()

    for j in range(1, 4):

        @pl.when(y < j)
        def _():
            both(xin.at[0], xsend.at[j]).wait()

    for k in range(2):

        @pl.when(core + 2 * k != x)
        def _():
            both(gp.at[k], osem.at[k]).wait()


def local(panel_pre, tail_panel, earlier, right_side, inverses):
    turns = panel_pre.shape[0]
    a = panel_pre.reshape(turns, 256, 256)
    b = tail_panel.reshape(256, 256)
    e = earlier.reshape(2, turns, 2, 128).transpose(1, 2, 0, 3).reshape(2 * turns, 2, 128)
    r = right_side.reshape(8, 4, 1, 256)
    g = inverses.reshape(256, 1024)
    hbm = pl.BlockSpec(memory_space=pltpu.HBM)
    vmem = pl.BlockSpec(memory_space=pltpu.VMEM)
    dma = pltpu.SemaphoreType.DMA
    out = pl.pallas_call(
        kernel,
        out_shape=jax.ShapeDtypeStruct((8, 4, 1, 256), F32),
        in_specs=[hbm] * 5,
        out_specs=vmem,
        scratch_shapes=[
            pltpu.VMEM((2 * turns, 2, 128), BF16),
            pltpu.VMEM((4, 1, 256), F32),
            pltpu.VMEM((turns, 256, 256), BF16),
            pltpu.VMEM((6, 256, 256), BF16),
            pltpu.VMEM((2, 256, 256), F32),
            pltpu.VMEM((2 * turns, 16, 2, 128), BF16),
            pltpu.VMEM((8, 4, 256), F32),
            pltpu.VMEM((16, 4, 256), F32),
            pltpu.VMEM((4, 256), F32),
            pltpu.VMEM((4, 256), F32),
            pltpu.VMEM((2, 4, 256), F32),
            pltpu.VMEM((3, 4, 2, 4, 256), F32),
            pltpu.VMEM((4, 4, 256), F32),
            pltpu.VMEM((4, 1, 256), F32),
            dma((CHUNKS + 6,)),
            dma((2,)),
            dma((1,)),
            dma((6,)),
            dma((2,)),
            dma((2,)),
            dma((4,)),
            dma((3,)),
            dma((3,)),
            dma((2,)),
        ],
        compiler_params=pltpu.CompilerParams(collective_id=0, has_side_effects=True, vmem_limit_bytes=64 << 20),
        cost_estimate=pl.CostEstimate(flops=2 * 32 * 256 * 256 * turns, bytes_accessed=6 << 20, transcendentals=0),
        name="solve",
    )(a, b, e, r, g)
    return out.reshape(32, 1, 1, 256)


def solution(mesh):
    in_specs = (
        P(None, "prow", None, None, "pcol", None),
        P(None, "prow", None, None, "pcol", None),
        P("pcol", None, "prow", None),
        P(None, None, "pcol", None),
        P(None, "pcol", None, None),
    )
    out_specs = P(None, None, "pcol", None)
    return jax.shard_map(local, mesh=mesh, in_specs=in_specs, out_specs=out_specs, check_vma=False)
```

time: 662 us -> 53.9 us (0.08)
  waiting for transfers between devices: 470 us -> 0 us
  blocking collectives: 155 us -> 0 us
  Pallas kernels: 0 us -> 52.3 us
  between operations: 13.3 us -> 0.01 us
  matrix products: 11.8 us -> 0 us
  other arithmetic: 7.51 us -> 0 us
    psum x5 -> x0, waiting for transfers between devices: 470 us -> none  [the longest x4 363 us: local(): block_x = lax.psum(partial_x, 'pcol')]
    psum x3 -> x0, blocking collectives: 136 us -> none  [local(): update = lax.psum(partial_update, 'prow')]
    pallas_call x0 -> x1, Pallas kernels: none -> 52.3 us  [local(): pl.pallas_call(kernel, out_shape=jax.ShapeDtypeStruct((8, 4, 1, 256), F32...]
    all_gather x1 -> x0, blocking collectives: 18.3 us -> none  [local(): lax.all_gather(known_rows, 'pcol', axis=0, tiled=True)]
    dot_general x9 -> x0, matrix products: 11.8 us -> none  [the longest x4 6.18 us: local(): partial_x = jnp.dot(masked, local_inv, precision=lax.Precision.HIGHEST)]
  transfers between devices with their start and end apart: 5 -> 0, of which waited for: 5 -> 0; matrix products, arithmetic and copies ran while one was open for 0% -> 0% of each run, Pallas kernels for 0% -> 0%
where the time goes in v1:
time: 53.9 us; the launch traced here: 53.7 us
  Pallas kernels  52.3 us (97%)
  local copies, waits for them, and re-layouts  1.38 us (3%)
    pallas_call x1, Pallas kernels, local(): pl.pallas_call(kernel, out_shape=jax.ShapeDtypeStruct((8, 4, 1, 256), F32...  52.3 us
    unnamed x1, local copies, waits for them, and re-layouts  1.38 us

profile of v1, /device:TPU:25, one launch (start us, length us, event | category | flops | bytes accessed | tf_op | source)
XLA Modules:
  0.0 53.7 jit_solution(13271037483286664696)
XLA Ops:
  0.0 52.3 %solve.1 = f32[8,4,1,256]{3,2,1,0:T(1,128)} custom-call(bf16[31,256,256]{2,1,0:T(8,128)(2,1)} %bitcast.12, bf16[256,256]{1,0:T(8,128)(2,1)} %bitcast.15, bf16[62,2,128]{2,1,0:T(2,128)(2,1)} %bitcast.17, f32[8,4,1,256]{3,2,1,0:T(1,128)} %bitcast.16, f32[256,1024]{1,0:T(8,128)} %bitcast.13), custom_call_target="tpu_custom_call" | custom-call | flops 130023424 | bytes 6291456 | tf_op jit(solution)/shard_map/solve/pallas_call | solution.py:205
  52.3 1.4 %copy.9 = f32[32,1,1,256]{3,2,1,0:T(1,128)} copy(f32[32,1,1,256]{3,2,1,0:T(1,128)} %bitcast.14) | data formatting | bytes 65536

commit v2 on v0

v2 whole, which is shorter than its diff:
```python
import jax
import jax.numpy as jnp
from jax import lax
from jax.experimental import pallas as pl
from jax.experimental.pallas import tpu as pltpu
from jax.sharding import PartitionSpec as P

MESH = pl.DeviceIdType.MESH
F32 = jnp.float32
BF16 = jnp.bfloat16
SPLIT = (0, 16, 31)


def kernel(a_hbm, b_hbm, e_hbm, r_hbm, g_hbm, o_ref, e_ref, r_ref, abuf, ball, gbuf, ghl, h, part, pin, upd, gp, xin, oin, ob, lsem, ysend, yrecv, bsend, brecv, psem, xsend, xrecv, osem, fsem):
    p = lax.axis_index("prow")
    col = lax.axis_index("pcol")
    z, core = p // 2, p % 2
    y, x = col // 4, col % 4
    solver = core == 1

    def both(ref, sem):
        return pltpu.make_async_copy(ref, ref, sem)

    def send(src, dst, ssem, rsem, to):
        pltpu.make_async_remote_copy(src, dst, ssem, rsem, device_id=to, device_id_type=MESH).start()

    load_y = pltpu.make_async_copy(e_hbm, e_ref, lsem.at[0])
    own_y = pltpu.make_async_copy(e_hbm, h.at[:, col], lsem.at[1])
    load_r = pltpu.make_async_copy(r_hbm.at[z], r_ref, lsem.at[2])
    load_g = pltpu.make_async_copy(g_hbm, gbuf, lsem.at[3])
    own_b = pltpu.make_async_copy(b_hbm, ball.at[p], lsem.at[4])
    chunks = [pl.ds(s, e - s) for s, e in zip(SPLIT, SPLIT[1:])]
    loads = [pltpu.make_async_copy(a_hbm.at[c], abuf.at[c], lsem.at[5 + i]) for i, c in enumerate(chunks)]
    has_b = p < 4 * y

    load_y.start()
    own_y.start()
    loads[0].start()

    @pl.when(solver)
    def _():
        load_g.start()
        load_r.start()

        @pl.when(has_b)
        def _():
            own_b.start()

    loads[1].start()

    barrier = pltpu.get_barrier_semaphore()
    for d in range(1, 16):
        pl.semaphore_signal(barrier, inc=1, device_id=(p, (col + d) % 16), device_id_type=MESH)
        pl.semaphore_signal(barrier, inc=1, device_id=((p + d) % 16, col), device_id_type=MESH)
    load_y.wait()
    pl.semaphore_wait(barrier, 30)

    for yy in range(4):
        for i, (s, e) in enumerate(zip(SPLIT, SPLIT[1:])):
            rows = pl.ds(2 * s, 2 * (e - s))
            for d in (1, 2, 3, 0):
                to = (p, 4 * yy + (x + d) % 4)

                def go():
                    send(e_ref.at[rows], h.at[rows, col], ysend, yrecv.at[i], to)

                if d:
                    go()
                else:
                    pl.when(y != yy)(go)

    def peer(d):
        return (2 * ((z + d) % 8) + 1, col)

    @pl.when(has_b)
    def _():
        send(b_hbm, ball.at[p], bsend, brecv.at[p], peer(1))
        send(b_hbm, ball.at[p], bsend, brecv.at[p], peer(7))

        @pl.when(jnp.logical_not(solver))
        def _():
            send(b_hbm, ball.at[p], bsend, brecv.at[p], peer(0))

    def tiles(s):
        return (z + s) % 8

    def await_tile(t):
        both(ball.at[t], brecv.at[t]).wait()

    def hand_on(s, d):
        src = tiles(s)

        @pl.when(jnp.logical_and(solver, src < 2 * y))
        def _():
            for k in range(2):
                t = 2 * src + k
                await_tile(t)
                send(ball.at[t], ball.at[t], bsend, brecv.at[t], peer(d))

    hand_on(-1, 1)
    hand_on(1, -1)

    @pl.when(solver)
    def _():
        load_g.wait()
        for t in range(4):
            g = gbuf[:, 256 * t : 256 * t + 256]
            hi = g.astype(BF16)
            ghl[t, :256] = hi
            ghl[t, 256:] = (g - hi.astype(F32)).astype(BF16)

    own_y.wait()
    acc = jnp.zeros((32, 256), F32)
    for i, (s, e) in enumerate(zip(SPLIT, SPLIT[1:])):
        loads[i].wait()
        both(h.at[pl.ds(2 * s, 2 * (e - s)), pl.ds(0, 15)], yrecv.at[i]).wait()
        for t in range(s, e):
            lhs = jnp.concatenate([h[2 * t].reshape(32, 128), h[2 * t + 1].reshape(32, 128)], axis=1)
            acc += jnp.dot(lhs, abuf[t], preferred_element_type=F32)
    part[...] = acc.reshape(8, 4, 256)

    for d in (4, 3, 5, 2, 6, 1, 7):
        to = (z + d) % 8
        send(part.at[to], pin.at[p], psem.at[0], psem.at[1], (2 * to + 1, col))

    @pl.when(jnp.logical_not(solver))
    def _():
        send(part.at[z], pin.at[p], psem.at[0], psem.at[1], (p + 1, col))

    hand_on(-2, 1)
    hand_on(2, -1)
    hand_on(-3, 1)

    @pl.when(solver)
    def _():
        pin[p] = part[z]
        for s in (3, 4):

            @pl.when(tiles(s) < 2 * y)
            def _():
                await_tile(2 * tiles(s))
                await_tile(2 * tiles(s) + 1)

        @pl.when(has_b)
        def _():
            await_tile(p - 1)
            own_b.wait()

        load_r.wait()
        both(pin.at[pl.ds(0, 15)], psem.at[1]).wait()
        upd[...] = r_ref[...].reshape(4, 256) - jnp.sum(pin[...], axis=0)

        for i in range(3):

            @pl.when(y > i)
            def _():
                both(xin.at[i], xrecv.at[i]).wait()
                solved = jnp.sum(xin[i], axis=0).astype(BF16)
                total = jnp.dot(solved[0], ball[4 * i], preferred_element_type=F32)
                for k in range(1, 4):
                    total += jnp.dot(solved[k], ball[4 * i + k], preferred_element_type=F32)
                upd[...] -= total

        remain = upd[...]
        low = remain - remain.astype(BF16).astype(F32)
        lhs = jnp.concatenate([remain, low], axis=0).astype(BF16)
        lhs = jnp.concatenate([lhs, lhs], axis=1)
        for t in range(4):
            res = jnp.dot(lhs, ghl[t], preferred_element_type=F32)
            gp[t] = res[:4] + res[4:]

        for j in range(1, 4):

            @pl.when(y < j)
            def _():
                for d in (2, 1, 3, 0):
                    send(gp, xin.at[y, x], xsend.at[j], xrecv.at[y], (p, 4 * j + (x + d) % 4))

        for d in (2, 1, 3):
            to = (x + d) % 4
            send(gp.at[to], oin.at[x], osem.at[0], osem.at[1], (p, 4 * y + to))
        oin[x] = gp[x]
        both(oin.at[pl.ds(0, 3)], osem.at[1]).wait()
        total = jnp.sum(oin[...], axis=0).reshape(4, 1, 256)
        ob[...] = total
        for d in (4, 3, 5, 2, 6, 1, 7):
            for k in range(2):
                send(ob, o_ref.at[z], fsem.at[0], fsem.at[1], (2 * ((z + d) % 8) + k, col))
        send(ob, o_ref.at[z], fsem.at[0], fsem.at[1], (p - 1, col))
        o_ref[z] = total
        both(o_ref.at[pl.ds(0, 7)], fsem.at[1]).wait()

        for j in range(1, 4):

            @pl.when(y < j)
            def _():
                both(xin.at[0], xsend.at[j]).wait()

        both(oin.at[pl.ds(0, 3)], osem.at[0]).wait()
        both(pin.at[pl.ds(0, 7)], psem.at[0]).wait()
        both(pin.at[pl.ds(0, 15)], fsem.at[0]).wait()
        for s in (-1, 1, -2, 2, -3):

            @pl.when(tiles(s) < 2 * y)
            def _():
                both(ball.at[pl.ds(0, 2)], bsend).wait()

        @pl.when(has_b)
        def _():
            both(ball.at[pl.ds(0, 2)], bsend).wait()

    @pl.when(jnp.logical_not(solver))
    def _():
        both(pin.at[pl.ds(0, 8)], psem.at[0]).wait()

        @pl.when(has_b)
        def _():
            both(ball.at[pl.ds(0, 3)], bsend).wait()

        both(o_ref, fsem.at[1]).wait()

    both(h.at[:, pl.ds(0, 15)], ysend).wait()


def local(panel_pre, tail_panel, earlier, right_side, inverses):
    turns = panel_pre.shape[0]
    a = panel_pre.reshape(turns, 256, 256)
    b = tail_panel.reshape(256, 256)
    e = earlier.reshape(2, turns, 2, 128).transpose(1, 2, 0, 3).reshape(2 * turns, 2, 128)
    r = right_side.reshape(8, 4, 1, 256)
    g = inverses.reshape(256, 1024)
    dma = pltpu.SemaphoreType.DMA
    out = pl.pallas_call(
        kernel,
        out_shape=jax.ShapeDtypeStruct((8, 4, 1, 256), F32),
        in_specs=[pl.BlockSpec(memory_space=pltpu.HBM)] * 5,
        out_specs=pl.BlockSpec(memory_space=pltpu.VMEM),
        scratch_shapes=[
            pltpu.VMEM((2 * turns, 2, 128), BF16),
            pltpu.VMEM((4, 1, 256), F32),
            pltpu.VMEM((turns, 256, 256), BF16),
            pltpu.VMEM((12, 256, 256), BF16),
            pltpu.VMEM((256, 1024), F32),
            pltpu.VMEM((4, 512, 256), BF16),
            pltpu.VMEM((2 * turns, 16, 2, 128), BF16),
            pltpu.VMEM((8, 4, 256), F32),
            pltpu.VMEM((16, 4, 256), F32),
            pltpu.VMEM((4, 256), F32),
            pltpu.VMEM((4, 4, 256), F32),
            pltpu.VMEM((3, 4, 4, 4, 256), F32),
            pltpu.VMEM((4, 4, 256), F32),
            pltpu.VMEM((4, 1, 256), F32),
            dma((7,)),
            dma,
            dma((2,)),
            dma,
            dma((12,)),
            dma((2,)),
            dma((4,)),
            dma((3,)),
            dma((2,)),
            dma((2,)),
        ],
        compiler_params=pltpu.CompilerParams(collective_id=0, has_side_effects=True, vmem_limit_bytes=64 << 20),
        cost_estimate=pl.CostEstimate(flops=2 * 32 * 256 * 256 * turns, bytes_accessed=6 << 20, transcendentals=0),
        name="solve",
    )(a, b, e, r, g)
    return out.reshape(32, 1, 1, 256)


def solution(mesh):
    in_specs = (
        P(None, "prow", None, None, "pcol", None),
        P(None, "prow", None, None, "pcol", None),
        P("pcol", None, "prow", None),
        P(None, None, "pcol", None),
        P(None, "pcol", None, None),
    )
    out_specs = P(None, None, "pcol", None)
    return jax.shard_map(local, mesh=mesh, in_specs=in_specs, out_specs=out_specs, check_vma=False)
```

time: 662 us -> 42.1 us (0.06)
  waiting for transfers between devices: 470 us -> 0 us
  blocking collectives: 155 us -> 0 us
  Pallas kernels: 0 us -> 40.6 us
  between operations: 13.3 us -> 0.01 us
  matrix products: 11.8 us -> 0 us
  other arithmetic: 7.51 us -> 0 us
    psum x5 -> x0, waiting for transfers between devices: 470 us -> none  [the longest x4 363 us: local(): block_x = lax.psum(partial_x, 'pcol')]
    psum x3 -> x0, blocking collectives: 136 us -> none  [local(): update = lax.psum(partial_update, 'prow')]
    pallas_call x0 -> x1, Pallas kernels: none -> 40.6 us  [local(): pl.pallas_call(kernel, out_shape=jax.ShapeDtypeStruct((8, 4, 1, 256), F32...]
    all_gather x1 -> x0, blocking collectives: 18.3 us -> none  [local(): lax.all_gather(known_rows, 'pcol', axis=0, tiled=True)]
    dot_general x9 -> x0, matrix products: 11.8 us -> none  [the longest x4 6.18 us: local(): partial_x = jnp.dot(masked, local_inv, precision=lax.Precision.HIGHEST)]
  transfers between devices with their start and end apart: 5 -> 0, of which waited for: 5 -> 0; matrix products, arithmetic and copies ran while one was open for 0% -> 0% of each run, Pallas kernels for 0% -> 0%
where the time goes in v2:
time: 42.1 us; the launch traced here: 42 us
  Pallas kernels  40.6 us (96%)
  local copies, waits for them, and re-layouts  1.38 us (3%)
    pallas_call x1, Pallas kernels, local(): pl.pallas_call(kernel, out_shape=jax.ShapeDtypeStruct((8, 4, 1, 256), F32...  40.6 us
    unnamed x1, local copies, waits for them, and re-layouts  1.38 us

profile of v2, /device:TPU:25, one launch (start us, length us, event | category | flops | bytes accessed | tf_op | source)
XLA Modules:
  0.0 42.0 jit_solution(11406337824653660335)
XLA Ops:
  0.0 40.6 %solve.1 = f32[8,4,1,256]{3,2,1,0:T(1,128)} custom-call(bf16[31,256,256]{2,1,0:T(8,128)(2,1)} %bitcast.12, bf16[256,256]{1,0:T(8,128)(2,1)} %bitcast.15, bf16[62,2,128]{2,1,0:T(2,128)(2,1)} %bitcast.17, f32[8,4,1,256]{3,2,1,0:T(1,128)} %bitcast.16, f32[256,1024]{1,0:T(8,128)} %bitcast.13), custom_call_target="tpu_custom_call" | custom-call | flops 130023424 | bytes 6291456 | tf_op jit(solution)/shard_map/solve/pallas_call | solution.py:233
  40.6 1.4 %copy.9 = f32[32,1,1,256]{3,2,1,0:T(1,128)} copy(f32[32,1,1,256]{3,2,1,0:T(1,128)} %bitcast.14) | data formatting | bytes 65536

commit v3 on v2

--- a/solution.py
+++ b/solution.py
@@ -9,6 +9,7 @@
 F32 = jnp.float32
 BF16 = jnp.bfloat16
 SPLIT = (0, 16, 31)
+LEVEL = (4, 5, 6, 7, 1, 0, 2, 3)
 
 
 def kernel(a_hbm, b_hbm, e_hbm, r_hbm, g_hbm, o_ref, e_ref, r_ref, abuf, ball, gbuf, ghl, h, part, pin, upd, gp, xin, oin, ob, lsem, ysend, yrecv, bsend, brecv, psem, xsend, xrecv, osem, fsem):
@@ -17,6 +18,7 @@
     z, core = p // 2, p % 2
     y, x = col // 4, col % 4
     solver = core == 1
+    group = sum(jnp.where(z == level, k, 0) for k, level in enumerate(LEVEL))
 
     def both(ref, sem):
         return pltpu.make_async_copy(ref, ref, sem)
@@ -26,7 +28,7 @@
 
     load_y = pltpu.make_async_copy(e_hbm, e_ref, lsem.at[0])
     own_y = pltpu.make_async_copy(e_hbm, h.at[:, col], lsem.at[1])
-    load_r = pltpu.make_async_copy(r_hbm.at[z], r_ref, lsem.at[2])
+    load_r = pltpu.make_async_copy(r_hbm.at[group], r_ref, lsem.at[2])
     load_g = pltpu.make_async_copy(g_hbm, gbuf, lsem.at[3])
     own_b = pltpu.make_async_copy(b_hbm, ball.at[p], lsem.at[4])
     chunks = [pl.ds(s, e - s) for s, e in zip(SPLIT, SPLIT[1:])]
@@ -62,7 +64,7 @@
                 to = (p, 4 * yy + (x + d) % 4)
 
                 def go():
-                    send(e_ref.at[rows], h.at[rows, col], ysend, yrecv.at[i], to)
+                    send(e_ref.at[rows], h.at[rows, col], ysend, yrecv.at[y // 2 * 2 + i], to)
 
                 if d:
                     go()
@@ -110,30 +112,42 @@
             ghl[t, 256:] = (g - hi.astype(F32)).astype(BF16)
 
     own_y.wait()
-    acc = jnp.zeros((32, 256), F32)
-    for i, (s, e) in enumerate(zip(SPLIT, SPLIT[1:])):
-        loads[i].wait()
-        both(h.at[pl.ds(2 * s, 2 * (e - s)), pl.ds(0, 15)], yrecv.at[i]).wait()
-        for t in range(s, e):
-            lhs = jnp.concatenate([h[2 * t].reshape(32, 128), h[2 * t + 1].reshape(32, 128)], axis=1)
-            acc += jnp.dot(lhs, abuf[t], preferred_element_type=F32)
-    part[...] = acc.reshape(8, 4, 256)
-
-    for d in (4, 3, 5, 2, 6, 1, 7):
-        to = (z + d) % 8
-        send(part.at[to], pin.at[p], psem.at[0], psem.at[1], (2 * to + 1, col))
-
-    @pl.when(jnp.logical_not(solver))
-    def _():
-        send(part.at[z], pin.at[p], psem.at[0], psem.at[1], (p + 1, col))
-
-    hand_on(-2, 1)
-    hand_on(2, -1)
+    for half in range(2):
+        acc = jnp.zeros((16, 256), F32)
+        for i, (s, e) in enumerate(zip(SPLIT, SPLIT[1:])):
+            if half == 0:
+                loads[i].wait()
+            rows, got = pl.ds(2 * s, 2 * (e - s)), yrecv.at[2 * half + i]
+
+            @pl.when(y // 2 == half)
+            def _():
+                both(h.at[rows, pl.ds(0, 7)], got).wait()
+
+            @pl.when(y // 2 != half)
+            def _():
+                both(h.at[rows, pl.ds(0, 8)], got).wait()
+
+            for t in range(s, e):
+                lhs = jnp.concatenate([h[2 * t + k, 8 * half : 8 * half + 8].reshape(16, 128) for k in range(2)], axis=1)
+                acc += jnp.dot(lhs, abuf[t], preferred_element_type=F32)
+        part[4 * half : 4 * half + 4] = acc.reshape(4, 4, 256)
+
+        for k in range(4 * half, 4 * half + 4):
+            to = 2 * LEVEL[k] + 1
+
+            @pl.when(p != to)
+            def _():
+                send(part.at[k], pin.at[p], psem.at[0], psem.at[1], (to, col))
+
+        if half == 0:
+            hand_on(-2, 1)
+            hand_on(2, -1)
+
     hand_on(-3, 1)
 
     @pl.when(solver)
     def _():
-        pin[p] = part[z]
+        pin[p] = part[group]
         for s in (3, 4):
 
             @pl.when(tiles(s) < 2 * y)
@@ -183,11 +197,13 @@
         both(oin.at[pl.ds(0, 3)], osem.at[1]).wait()
         total = jnp.sum(oin[...], axis=0).reshape(4, 1, 256)
         ob[...] = total
-        for d in (4, 3, 5, 2, 6, 1, 7):
-            for k in range(2):
-                send(ob, o_ref.at[z], fsem.at[0], fsem.at[1], (2 * ((z + d) % 8) + k, col))
-        send(ob, o_ref.at[z], fsem.at[0], fsem.at[1], (p - 1, col))
-        o_ref[z] = total
+        for to in (1, 0, 3, 2, 5, 4, 7, 6, 15, 14, 9, 8, 13, 12, 11, 10):
+
+            @pl.when(p != to)
+            def _():
+                send(ob, o_ref.at[group], fsem.at[0], fsem.at[1], (to, col))
+
+        o_ref[group] = total
         both(o_ref.at[pl.ds(0, 7)], fsem.at[1]).wait()
 
         for j in range(1, 4):
@@ -252,7 +268,7 @@
             pltpu.VMEM((4, 1, 256), F32),
             dma((7,)),
             dma,
-            dma((2,)),
+            dma((4,)),
             dma,
             dma((12,)),
             dma((2,)),

time: 42.1 us -> 41.1 us (0.976)
  Pallas kernels: 40.6 us -> 39.5 us
    pallas_call x1, Pallas kernels: 40.6 us -> 39.5 us  [local(): pl.pallas_call(kernel, out_shape=jax.ShapeDtypeStruct((8, 4, 1, 256), F32...]
where the time goes in v3:
time: 41.1 us; the launch traced here: 40.9 us
  Pallas kernels  39.5 us (96%)
  local copies, waits for them, and re-layouts  1.38 us (3%)
    pallas_call x1, Pallas kernels, local(): pl.pallas_call(kernel, out_shape=jax.ShapeDtypeStruct((8, 4, 1, 256), F32...  39.5 us
    unnamed x1, local copies, waits for them, and re-layouts  1.38 us

profile of v3, /device:TPU:25, one launch (start us, length us, event | category | flops | bytes accessed | tf_op | source)
XLA Modules:
  0.0 40.9 jit_solution(17226339815907361200)
XLA Ops:
  0.0 39.5 %solve.1 = f32[8,4,1,256]{3,2,1,0:T(1,128)} custom-call(bf16[31,256,256]{2,1,0:T(8,128)(2,1)} %bitcast.12, bf16[256,256]{1,0:T(8,128)(2,1)} %bitcast.15, bf16[62,2,128]{2,1,0:T(2,128)(2,1)} %bitcast.17, f32[8,4,1,256]{3,2,1,0:T(1,128)} %bitcast.16, f32[256,1024]{1,0:T(8,128)} %bitcast.13), custom_call_target="tpu_custom_call" | custom-call | flops 130023424 | bytes 6291456 | tf_op jit(solution)/shard_map/solve/pallas_call | solution.py:249
  39.5 1.4 %copy.9 = f32[32,1,1,256]{3,2,1,0:T(1,128)} copy(f32[32,1,1,256]{3,2,1,0:T(1,128)} %bitcast.14) | data formatting | bytes 65536

commit v4 on v3

--- a/solution.py
+++ b/solution.py
@@ -12,7 +12,7 @@
 LEVEL = (4, 5, 6, 7, 1, 0, 2, 3)
 
 
-def kernel(a_hbm, b_hbm, e_hbm, r_hbm, g_hbm, o_ref, e_ref, r_ref, abuf, ball, gbuf, ghl, h, part, pin, upd, gp, xin, oin, ob, lsem, ysend, yrecv, bsend, brecv, psem, xsend, xrecv, osem, fsem):
+def kernel(a_hbm, b_hbm, e_hbm, r_hbm, g_hbm, o_ref, e_ref, r_ref, abuf, ball, gbuf, ghl, h, part, pin, upd, gp, xin, oin, ob, lsem, ysend, yrecv, bsend, brecv, psem, xsend, xrecv, osem, fsem, tok):
     p = lax.axis_index("prow")
     col = lax.axis_index("pcol")
     z, core = p // 2, p % 2
@@ -50,12 +50,44 @@
 
     loads[1].start()
 
+    def peer(d):
+        return (2 * ((z + d) % 8) + 1, col)
+
+    def signal(sem, to):
+        pl.semaphore_signal(sem, inc=1, device_id=to, device_id_type=MESH)
+
     barrier = pltpu.get_barrier_semaphore()
-    for d in range(1, 16):
-        pl.semaphore_signal(barrier, inc=1, device_id=(p, (col + d) % 16), device_id_type=MESH)
-        pl.semaphore_signal(barrier, inc=1, device_id=((p + d) % 16, col), device_id_type=MESH)
+    for dy in (2, 1, 3, 0):
+        for dx in (2, 1, 3, 0):
+            if dy or dx:
+                signal(barrier, (p, (y + dy) % 4 * 4 + (x + dx) % 4))
+
+    signal(barrier, (p + 1 - 2 * core, col))
+
+    @pl.when(core == 1)
+    def _():
+        for d in (1, 7):
+            for k in range(2):
+                signal(barrier, (2 * ((z + d) % 8) + k, col))
+
     load_y.wait()
-    pl.semaphore_wait(barrier, 30)
+    pl.semaphore_wait(barrier, 18)
+
+    def hear(up, down):
+        @pl.when(core == 1)
+        def _():
+            pl.semaphore_wait(tok.at[0], 1)
+            if up:
+                signal(tok.at[0], peer(1))
+            if down is not None:
+                pl.semaphore_wait(tok.at[1], 1)
+            if down:
+                signal(tok.at[1], peer(7))
+
+    @pl.when(core == 1)
+    def _():
+        signal(tok.at[0], peer(1))
+        signal(tok.at[1], peer(7))
 
     for yy in range(4):
         for i, (s, e) in enumerate(zip(SPLIT, SPLIT[1:])):
@@ -71,9 +103,6 @@
                 else:
                     pl.when(y != yy)(go)
 
-    def peer(d):
-        return (2 * ((z + d) % 8) + 1, col)
-
     @pl.when(has_b)
     def _():
         send(b_hbm, ball.at[p], bsend, brecv.at[p], peer(1))
@@ -99,8 +128,10 @@
                 await_tile(t)
                 send(ball.at[t], ball.at[t], bsend, brecv.at[t], peer(d))
 
+    hear(True, True)
     hand_on(-1, 1)
     hand_on(1, -1)
+    hear(True, False)
 
     @pl.when(solver)
     def _():
@@ -112,6 +143,12 @@
             ghl[t, 256:] = (g - hi.astype(F32)).astype(BF16)
 
     own_y.wait()
+    hear(False, None)
+
+    @pl.when(core == 1)
+    def _():
+        signal(tok.at[2], (p - 1, col))
+
     for half in range(2):
         acc = jnp.zeros((16, 256), F32)
         for i, (s, e) in enumerate(zip(SPLIT, SPLIT[1:])):
@@ -131,6 +168,12 @@
                 lhs = jnp.concatenate([h[2 * t + k, 8 * half : 8 * half + 8].reshape(16, 128) for k in range(2)], axis=1)
                 acc += jnp.dot(lhs, abuf[t], preferred_element_type=F32)
         part[4 * half : 4 * half + 4] = acc.reshape(4, 4, 256)
+
+        if half == 0:
+
+            @pl.when(core == 0)
+            def _():
+                pl.semaphore_wait(tok.at[2], 1)
 
         for k in range(4 * half, 4 * half + 4):
             to = 2 * LEVEL[k] + 1
@@ -276,6 +319,7 @@
             dma((3,)),
             dma((2,)),
             dma((2,)),
+            pltpu.SemaphoreType.REGULAR((3,)),
         ],
         compiler_params=pltpu.CompilerParams(collective_id=0, has_side_effects=True, vmem_limit_bytes=64 << 20),
         cost_estimate=pl.CostEstimate(flops=2 * 32 * 256 * 256 * turns, bytes_accessed=6 << 20, transcendentals=0),

time: 41.1 us -> 40.1 us (0.976)
  Pallas kernels: 39.5 us -> 38.6 us
    pallas_call x1, Pallas kernels: 39.5 us -> 38.6 us  [local(): pl.pallas_call(kernel, out_shape=jax.ShapeDtypeStruct((8, 4, 1, 256), F32...]
where the time goes in v4:
time: 40.1 us; the launch traced here: 40 us
  Pallas kernels  38.6 us (96%)
  local copies, waits for them, and re-layouts  1.38 us (3%)
    pallas_call x1, Pallas kernels, local(): pl.pallas_call(kernel, out_shape=jax.ShapeDtypeStruct((8, 4, 1, 256), F32...  38.6 us
    unnamed x1, local copies, waits for them, and re-layouts  1.38 us

profile of v4, /device:TPU:25, one launch (start us, length us, event | category | flops | bytes accessed | tf_op | source)
XLA Modules:
  0.0 40.0 jit_solution(10220131145724774404)
XLA Ops:
  0.0 38.6 %solve.1 = f32[8,4,1,256]{3,2,1,0:T(1,128)} custom-call(bf16[31,256,256]{2,1,0:T(8,128)(2,1)} %bitcast.12, bf16[256,256]{1,0:T(8,128)(2,1)} %bitcast.15, bf16[62,2,128]{2,1,0:T(2,128)(2,1)} %bitcast.17, f32[8,4,1,256]{3,2,1,0:T(1,128)} %bitcast.16, f32[256,1024]{1,0:T(8,128)} %bitcast.13), custom_call_target="tpu_custom_call" | custom-call | flops 130023424 | bytes 6291456 | tf_op jit(solution)/shard_map/solve/pallas_call | solution.py:292
  38.6 1.4 %copy.9 = f32[32,1,1,256]{3,2,1,0:T(1,128)} copy(f32[32,1,1,256]{3,2,1,0:T(1,128)} %bitcast.14) | data formatting | bytes 65536

commit v5 on v4

--- a/solution.py
+++ b/solution.py
@@ -9,7 +9,7 @@
 F32 = jnp.float32
 BF16 = jnp.bfloat16
 SPLIT = (0, 16, 31)
-LEVEL = (4, 5, 6, 7, 1, 0, 2, 3)
+LEVEL = (4, 3, 5, 2, 0, 7, 6, 1)
 
 
 def kernel(a_hbm, b_hbm, e_hbm, r_hbm, g_hbm, o_ref, e_ref, r_ref, abuf, ball, gbuf, ghl, h, part, pin, upd, gp, xin, oin, ob, lsem, ysend, yrecv, bsend, brecv, psem, xsend, xrecv, osem, fsem, tok):
@@ -92,7 +92,7 @@
     for yy in range(4):
         for i, (s, e) in enumerate(zip(SPLIT, SPLIT[1:])):
             rows = pl.ds(2 * s, 2 * (e - s))
-            for d in (1, 2, 3, 0):
+            for d in (2, 1, 3, 0):
                 to = (p, 4 * yy + (x + d) % 4)
 
                 def go():

time: 40.1 us -> 39.4 us (0.983)
  Pallas kernels: 38.6 us -> 37.8 us
    pallas_call x1, Pallas kernels: 38.6 us -> 37.8 us  [local(): pl.pallas_call(kernel, out_shape=jax.ShapeDtypeStruct((8, 4, 1, 256), F32...]
where the time goes in v5:
time: 39.4 us; the launch traced here: 39.2 us
  Pallas kernels  37.8 us (96%)
  local copies, waits for them, and re-layouts  1.38 us (4%)
    pallas_call x1, Pallas kernels, local(): pl.pallas_call(kernel, out_shape=jax.ShapeDtypeStruct((8, 4, 1, 256), F32...  37.8 us
    unnamed x1, local copies, waits for them, and re-layouts  1.38 us

profile of v5, /device:TPU:25, one launch (start us, length us, event | category | flops | bytes accessed | tf_op | source)
XLA Modules:
  0.0 39.2 jit_solution(16483451092654001820)
XLA Ops:
  0.0 37.8 %solve.1 = f32[8,4,1,256]{3,2,1,0:T(1,128)} custom-call(bf16[31,256,256]{2,1,0:T(8,128)(2,1)} %bitcast.12, bf16[256,256]{1,0:T(8,128)(2,1)} %bitcast.15, bf16[62,2,128]{2,1,0:T(2,128)(2,1)} %bitcast.17, f32[8,4,1,256]{3,2,1,0:T(1,128)} %bitcast.16, f32[256,1024]{1,0:T(8,128)} %bitcast.13), custom_call_target="tpu_custom_call" | custom-call | flops 130023424 | bytes 6291456 | tf_op jit(solution)/shard_map/solve/pallas_call | solution.py:292
  37.8 1.4 %copy.9 = f32[32,1,1,256]{3,2,1,0:T(1,128)} copy(f32[32,1,1,256]{3,2,1,0:T(1,128)} %bitcast.14) | data formatting | bytes 65536

commit v6 on v5

--- a/solution.py
+++ b/solution.py
@@ -64,14 +64,16 @@
 
     signal(barrier, (p + 1 - 2 * core, col))
 
-    @pl.when(core == 1)
-    def _():
-        for d in (1, 7):
+    for d, start in ((1, 7), (7, 4)):
+
+        @pl.when(jnp.logical_and(core == 1, z != start))
+        def _():
             for k in range(2):
                 signal(barrier, (2 * ((z + d) % 8) + k, col))
 
     load_y.wait()
-    pl.semaphore_wait(barrier, 18)
+    edge = jnp.logical_or(z == 0, z == 3)
+    pl.semaphore_wait(barrier, jnp.where(edge, 17, 18))
 
     def hear(up, down):
         @pl.when(core == 1)
@@ -84,10 +86,19 @@
             if down:
                 signal(tok.at[1], peer(7))
 
-    @pl.when(core == 1)
-    def _():
+    def first_word():
         signal(tok.at[0], peer(1))
         signal(tok.at[1], peer(7))
+
+    for d, start in ((1, 7), (7, 4)):
+
+        @pl.when(jnp.logical_and(core == 1, z == start))
+        def _():
+            signal(tok.at[3], peer(d))
+
+    @pl.when(jnp.logical_and(core == 1, jnp.logical_not(edge)))
+    def _():
+        first_word()
 
     for yy in range(4):
         for i, (s, e) in enumerate(zip(SPLIT, SPLIT[1:])):
@@ -103,14 +114,27 @@
                 else:
                     pl.when(y != yy)(go)
 
-    @pl.when(has_b)
-    def _():
-        send(b_hbm, ball.at[p], bsend, brecv.at[p], peer(1))
-        send(b_hbm, ball.at[p], bsend, brecv.at[p], peer(7))
-
-        @pl.when(jnp.logical_not(solver))
-        def _():
-            send(b_hbm, ball.at[p], bsend, brecv.at[p], peer(0))
+    def spread(d, when):
+        @pl.when(jnp.logical_and(has_b, when))
+        def _():
+            send(b_hbm, ball.at[p], bsend, brecv.at[p], peer(d))
+
+    spread(1, z != 3)
+    spread(7, z != 0)
+    spread(0, core == 0)
+
+    @pl.when(jnp.logical_and(core == 1, edge))
+    def _():
+        pl.semaphore_wait(tok.at[3], 1)
+        signal(tok.at[3], (p - 1, col))
+        first_word()
+
+    @pl.when(jnp.logical_and(core == 0, edge))
+    def _():
+        pl.semaphore_wait(tok.at[3], 1)
+
+    spread(1, z == 3)
+    spread(7, z == 0)
 
     def tiles(s):
         return (z + s) % 8
@@ -128,9 +152,9 @@
                 await_tile(t)
                 send(ball.at[t], ball.at[t], bsend, brecv.at[t], peer(d))
 
-    hear(True, True)
     hand_on(-1, 1)
     hand_on(1, -1)
+    hear(True, True)
     hear(True, False)
 
     @pl.when(solver)
@@ -319,7 +343,7 @@
             dma((3,)),
             dma((2,)),
             dma((2,)),
-            pltpu.SemaphoreType.REGULAR((3,)),
+            pltpu.SemaphoreType.REGULAR((4,)),
         ],
         compiler_params=pltpu.CompilerParams(collective_id=0, has_side_effects=True, vmem_limit_bytes=64 << 20),
         cost_estimate=pl.CostEstimate(flops=2 * 32 * 256 * 256 * turns, bytes_accessed=6 << 20, transcendentals=0),

time: 39.4 us -> 39.2 us (level)
  no operation moved by 1% of the time
where the time goes in v6:
time: 39.2 us; the launch traced here: 39 us
  Pallas kernels  37.6 us (96%)
  local copies, waits for them, and re-layouts  1.38 us (4%)
    pallas_call x1, Pallas kernels, local(): pl.pallas_call(kernel, out_shape=jax.ShapeDtypeStruct((8, 4, 1, 256), F32...  37.6 us
    unnamed x1, local copies, waits for them, and re-layouts  1.38 us

profile of v6, /device:TPU:25, one launch (start us, length us, event | category | flops | bytes accessed | tf_op | source)
XLA Modules:
  0.0 39.0 jit_solution(4769696730250203820)
XLA Ops:
  0.0 37.6 %solve.1 = f32[8,4,1,256]{3,2,1,0:T(1,128)} custom-call(bf16[31,256,256]{2,1,0:T(8,128)(2,1)} %bitcast.12, bf16[256,256]{1,0:T(8,128)(2,1)} %bitcast.15, bf16[62,2,128]{2,1,0:T(2,128)(2,1)} %bitcast.17, f32[8,4,1,256]{3,2,1,0:T(1,128)} %bitcast.16, f32[256,1024]{1,0:T(8,128)} %bitcast.13), custom_call_target="tpu_custom_call" | custom-call | flops 130023424 | bytes 6291456 | tf_op jit(solution)/shard_map/solve/pallas_call | solution.py:316
  37.6 1.4 %copy.9 = f32[32,1,1,256]{3,2,1,0:T(1,128)} copy(f32[32,1,1,256]{3,2,1,0:T(1,128)} %bitcast.14) | data formatting | bytes 65536

commit v7 on v6

--- a/solution.py
+++ b/solution.py
@@ -152,9 +152,9 @@
                 await_tile(t)
                 send(ball.at[t], ball.at[t], bsend, brecv.at[t], peer(d))
 
+    hear(True, True)
     hand_on(-1, 1)
     hand_on(1, -1)
-    hear(True, True)
     hear(True, False)
 
     @pl.when(solver)

time: 39.2 us -> 39 us (level)
  no operation moved by 1% of the time
where the time goes in v7:
time: 39 us; the launch traced here: 38.9 us
  Pallas kernels  37.5 us (96%)
  local copies, waits for them, and re-layouts  1.38 us (4%)
    pallas_call x1, Pallas kernels, local(): pl.pallas_call(kernel, out_shape=jax.ShapeDtypeStruct((8, 4, 1, 256), F32...  37.5 us
    unnamed x1, local copies, waits for them, and re-layouts  1.38 us

profile of v7, /device:TPU:25, one launch (start us, length us, event | category | flops | bytes accessed | tf_op | source)
XLA Modules:
  0.0 38.9 jit_solution(12569342263359948372)
XLA Ops:
  0.0 37.5 %solve.1 = f32[8,4,1,256]{3,2,1,0:T(1,128)} custom-call(bf16[31,256,256]{2,1,0:T(8,128)(2,1)} %bitcast.12, bf16[256,256]{1,0:T(8,128)(2,1)} %bitcast.15, bf16[62,2,128]{2,1,0:T(2,128)(2,1)} %bitcast.17, f32[8,4,1,256]{3,2,1,0:T(1,128)} %bitcast.16, f32[256,1024]{1,0:T(8,128)} %bitcast.13), custom_call_target="tpu_custom_call" | custom-call | flops 130023424 | bytes 6291456 | tf_op jit(solution)/shard_map/solve/pallas_call | solution.py:316
  37.5 1.4 %copy.9 = f32[32,1,1,256]{3,2,1,0:T(1,128)} copy(f32[32,1,1,256]{3,2,1,0:T(1,128)} %bitcast.14) | data formatting | bytes 65536

commit v8 on v7

--- a/solution.py
+++ b/solution.py
@@ -199,7 +199,7 @@
             def _():
                 pl.semaphore_wait(tok.at[2], 1)
 
-        for k in range(4 * half, 4 * half + 4):
+        for k in ((0, 2, 1, 3), (7, 4, 5, 6))[half]:
             to = 2 * LEVEL[k] + 1
 
             @pl.when(p != to)

time: 39 us -> 39 us (level)
  no operation moved by 1% of the time
where the time goes in v8:
time: 39 us; the launch traced here: 38.8 us
  Pallas kernels  37.5 us (96%)
  local copies, waits for them, and re-layouts  1.38 us (4%)
    pallas_call x1, Pallas kernels, local(): pl.pallas_call(kernel, out_shape=jax.ShapeDtypeStruct((8, 4, 1, 256), F32...  37.5 us
    unnamed x1, local copies, waits for them, and re-layouts  1.38 us

profile of v8, /device:TPU:25, one launch (start us, length us, event | category | flops | bytes accessed | tf_op | source)
XLA Modules:
  0.0 38.8 jit_solution(16141898887368985699)
XLA Ops:
  0.0 37.5 %solve.1 = f32[8,4,1,256]{3,2,1,0:T(1,128)} custom-call(bf16[31,256,256]{2,1,0:T(8,128)(2,1)} %bitcast.12, bf16[256,256]{1,0:T(8,128)(2,1)} %bitcast.15, bf16[62,2,128]{2,1,0:T(2,128)(2,1)} %bitcast.17, f32[8,4,1,256]{3,2,1,0:T(1,128)} %bitcast.16, f32[256,1024]{1,0:T(8,128)} %bitcast.13), custom_call_target="tpu_custom_call" | custom-call | flops 130023424 | bytes 6291456 | tf_op jit(solution)/shard_map/solve/pallas_call | solution.py:316
  37.5 1.4 %copy.9 = f32[32,1,1,256]{3,2,1,0:T(1,128)} copy(f32[32,1,1,256]{3,2,1,0:T(1,128)} %bitcast.14) | data formatting | bytes 65536
